TPU v7x, 128 devices: a whole 4x4x4 slice. The times are simulated.
128 devices in a mesh: tok: 32 (over z, y_lo, x), head: 4 (over y_hi, core).
Axes of the slice: x: 4, y: 4 (y_hi: 2, y_lo: 2; y = y_hi * 2 + y_lo), z: 4, core: 2. Of those that a mesh axis runs over, the one named last changes fastest.
Arguments:
- queries: bfloat16 [32768, 8192], P('tok', 'head'), may hold values from -12 to 12
- keys: bfloat16 [32768, 1024], P('tok', 'head'), may hold values from -12 to 12
- values: bfloat16 [32768, 1024], P('tok', 'head'), may hold values from -6 to 6
- tile_docs: int32 [256], P('tok'), may hold values from 0 to 255, as said below
Outputs:
- attention: bfloat16 [32768, 8192], P(('tok', 'head'))
Inputs may be any that keep to these rules, and one draw needn't show every extreme that they name: `tile_docs`: each tile holds the index of the first tile of its document, so numbers never fall and are equal exactly within a document; tile 0 and the last tile each begin a document; every block of 8 tiles along tok holds the first tile of some document after its own first tile, so that a document lies within the blocks of at most two neighbouring indices of tok. The block of an even index of tok begins with a document; the block of an odd index never does, so its first document reaches back into the previous block.
All inputs are finite; a program needn't handle non-finite values.
Results may differ from a plain program's by a relative error of at most 0.004.
Values may be sent and summed in bfloat16 or wider, within the bound.
A program may use at most 128 MiB of HBM per device.

v0:
```python
import functools

import jax
import jax.numpy as jnp
from jax import lax
from jax.experimental import pallas as pl
from jax.experimental.pallas import tpu as pltpu
from jax.sharding import PartitionSpec as P

HEAD_DIM = 128
QPK = 8
TILE = 128
MESH = pl.DeviceIdType.MESH
HIDDEN = -1e30
EXPONENT_SCALE = HEAD_DIM**-0.5 * 1.4426950408889634
STACK = 2
CHUNK = 256


def kernel(docs, q_hbm, k_hbm, v_hbm, out, q, keys, vals, bias, stage,
           q_sem, kv_sem, rim_send, rim_recv, send_sem, recv_sem, own_sem):
    tok, head = lax.axis_index("tok"), lax.axis_index("head")
    y_hi, core = head // 2, head % 2
    odd = tok % 2
    sibling = (tok, 2 * y_hi + 1 - core)
    across = [(tok, 2 * (1 - y_hi) + c) for c in range(2)]
    neighbour = (tok + 1 - 2 * odd, head)

    barrier = pltpu.get_barrier_semaphore()
    for device in (sibling, *across, neighbour):
        pl.semaphore_signal(barrier, inc=1, device_id=device, device_id_type=MESH)

    far, near = 4 * (1 - y_hi), 4 * y_hi

    def load_q(part):
        first = pl.multiple_of(jnp.where(part == 0, far, near) * TILE, 4 * TILE)
        rows = pl.ds(first, 4 * TILE)
        return pltpu.make_async_copy(q_hbm.at[rows], q.at[rows], q_sem.at[part])

    def load_kv(g):
        source = (slice(None), pl.ds(g * HEAD_DIM, HEAD_DIM))
        target = (g, pl.ds(7 * TILE, 8 * TILE))
        return (
            pltpu.make_async_copy(k_hbm.at[source], keys.at[target], kv_sem.at[0, g]),
            pltpu.make_async_copy(v_hbm.at[source], vals.at[target], kv_sem.at[1, g]),
        )

    def rim(g):
        source = (pl.ds(TILE, 7 * TILE), pl.ds(g * HEAD_DIM, HEAD_DIM))
        target = (g, pl.ds(0, 7 * TILE))
        return [
            pltpu.make_async_remote_copy(
                src_ref=here.at[source], dst_ref=there.at[target],
                send_sem=rim_send.at[which, g], recv_sem=rim_recv.at[which, g],
                device_id=neighbour, device_id_type=MESH,
            )
            for which, (here, there) in enumerate(((k_hbm, keys), (v_hbm, vals)))
        ]

    for copy in load_kv(0):
        copy.start()
    load_q(0).start()
    for copy in load_kv(1):
        copy.start()
    load_q(1).start()

    blank = jnp.zeros((TILE, HEAD_DIM), jnp.bfloat16)
    for g in range(2):
        keys[g, 15 * TILE :] = blank
        vals[g, 15 * TILE :] = blank

    @pl.when(odd == 0)
    def _():
        for g in range(2):
            keys[g, 6 * TILE : 7 * TILE] = blank
            vals[g, 6 * TILE : 7 * TILE] = blank

    pl.semaphore_wait(barrier, 4)

    @pl.when(odd == 0)
    def _():
        for g in range(2):
            for copy in rim(g):
                copy.start()

    eye = (
        lax.broadcasted_iota(jnp.int32, (TILE, TILE), 0)
        == lax.broadcasted_iota(jnp.int32, (TILE, TILE), 1)
    ).astype(jnp.float32).astype(jnp.bfloat16)

    def attend(i, g, t, first, chunks):
        length = chunks * CHUNK
        span = pl.ds(pl.multiple_of(first * CHUNK, CHUNK), length)
        rows = pl.ds(pl.multiple_of(t * TILE, TILE), TILE)

        def group(j, carry):
            base = pl.multiple_of((g * QPK + j * STACK) * HEAD_DIM, STACK * HEAD_DIM)
            wide = q[rows, pl.ds(base, STACK * HEAD_DIM)]
            queries = jnp.concatenate(
                [
                    jnp.concatenate([wide[:, a * HEAD_DIM : (a + 1) * HEAD_DIM], eye], 1)
                    for a in range(STACK)
                ],
                0,
            )
            known = jnp.concatenate([keys[g, span], bias[span]], 1)
            scores = lax.dot_general(
                queries, known, (((1,), (1,)), ((), ())), preferred_element_type=jnp.float32
            )
            maxima = jnp.max(scores, axis=1, keepdims=True)
            weights = jnp.exp2((scores - maxima) * EXPONENT_SCALE).astype(jnp.bfloat16)
            summed = jnp.dot(
                weights,
                jnp.concatenate(
                    [vals[g, span], jnp.ones((length, HEAD_DIM), jnp.bfloat16)], 1
                ),
                preferred_element_type=jnp.float32,
            )
            result = (summed[:, :HEAD_DIM] / summed[:, HEAD_DIM:]).astype(jnp.bfloat16)
            stage[i, :, pl.ds(pl.multiple_of(j * STACK * HEAD_DIM, STACK * HEAD_DIM), STACK * HEAD_DIM)] = (
                jnp.concatenate([result[a * TILE : (a + 1) * TILE] for a in range(STACK)], 1)
            )
            return carry

        lax.fori_loop(0, QPK // STACK, group, 0)

    def place(i):
        crossing = i < 8
        g = jnp.where(crossing, i // 4, (i // 2) % 2)
        t = jnp.where(
            crossing, far + i % 4, near + 2 * jnp.where(i < 12, 1 - core, core) + i % 2
        )
        return g, t

    def send(i):
        g, t = place(i)
        return pltpu.make_async_remote_copy(
            src_ref=stage.at[i],
            dst_ref=out.at[
                pl.ds(pl.multiple_of((t % 2) * TILE, TILE), TILE),
                pl.ds(pl.multiple_of((head * 2 + g) * QPK * HEAD_DIM, QPK * HEAD_DIM), QPK * HEAD_DIM),
            ],
            send_sem=send_sem.at[i],
            recv_sem=recv_sem.at[head, g, t % 2],
            device_id=(tok, t // 2),
            device_id_type=MESH,
        )

    def keep(i):
        g, t = place(i)
        return pltpu.make_async_copy(
            stage.at[i],
            out.at[
                pl.ds(pl.multiple_of((t % 2) * TILE, TILE), TILE),
                pl.ds(pl.multiple_of((head * 2 + g) * QPK * HEAD_DIM, QPK * HEAD_DIM), QPK * HEAD_DIM),
            ],
            own_sem.at[i - 12],
        )

    def unit(i, carry):
        g, t = place(i)

        @pl.when(i % 4 == 0)
        def _():
            @pl.when(i < 8)
            def _():
                for copy in load_kv(i // 4):
                    copy.wait()

                @pl.when(odd == 1)
                def _():
                    for copy in rim(i // 4):
                        copy.wait_recv()

            @pl.when(i == 0)
            def _():
                load_q(0).wait()

            @pl.when(i == 8)
            def _():
                load_q(1).wait()

        reaches_back = jnp.where(t == 7, 0, odd)
        first = 3 - 3 * reaches_back
        count = (7 + t) // 2 + 1 - first
        begin = (docs[t] - 8 * tok + 7) * TILE
        row = lax.broadcasted_iota(jnp.int32, (CHUNK, TILE), 1) + (7 + t) * TILE

        def hide(c, carry):
            at = pl.multiple_of((first + c) * CHUNK, CHUNK)
            key = lax.broadcasted_iota(jnp.int32, (CHUNK, TILE), 0) + at
            bias[pl.ds(at, CHUNK)] = jnp.where(
                (key >= begin) & (key <= row), 0.0, HIDDEN
            ).astype(jnp.bfloat16)
            return carry

        lax.fori_loop(0, count, hide, 0)

        for chunks in range(1, 8):
            @pl.when(count == chunks)
            def _(chunks=chunks):
                attend(i, g, t, first, chunks)

        @pl.when(i < 12)
        def _():
            send(i).start()

        @pl.when(i >= 12)
        def _():
            keep(i).start()

        return carry

    lax.fori_loop(0, 16, unit, 0)

    @pl.when(odd == 0)
    def _():
        for g in range(2):
            for copy in rim(g):
                copy.wait_send()

    def finish(i, carry):
        send(i).wait_send()
        return carry

    lax.fori_loop(0, 12, finish, 0)
    for i in range(12, 16):
        keep(i).wait()

    def arrive(n, carry):
        other = (head + 1 + n // 4) % 4
        g, half = (n // 2) % 2, n % 2
        piece = out.at[
            pl.ds(pl.multiple_of(half * TILE, TILE), TILE),
            pl.ds(pl.multiple_of((other * 2 + g) * QPK * HEAD_DIM, QPK * HEAD_DIM), QPK * HEAD_DIM),
        ]
        pltpu.make_async_remote_copy(
            src_ref=stage.at[0], dst_ref=piece, send_sem=send_sem.at[0],
            recv_sem=recv_sem.at[other, g, half], device_id=sibling, device_id_type=MESH,
        ).wait_recv()
        return carry

    lax.fori_loop(0, 12, arrive, 0)


def local(queries, keys, values, tile_docs):
    rows, width = queries.shape
    kv_width = keys.shape[1]
    groups = kv_width // HEAD_DIM
    heads = lax.axis_size("head")
    flops = 2 * 2 * 60 * TILE * TILE * width
    return pl.pallas_call(
        kernel,
        out_shape=jax.ShapeDtypeStruct((rows // heads, width * heads), jnp.bfloat16),
        in_specs=[pl.BlockSpec(memory_space=pltpu.SMEM)] + [pl.BlockSpec(memory_space=pl.ANY)] * 3,
        out_specs=pl.BlockSpec(memory_space=pl.ANY),
        scratch_shapes=[
            pltpu.VMEM((rows, width), jnp.bfloat16),
            pltpu.VMEM((groups, 2 * rows, HEAD_DIM), jnp.bfloat16),
            pltpu.VMEM((groups, 2 * rows, HEAD_DIM), jnp.bfloat16),
            pltpu.VMEM((2 * rows, TILE), jnp.bfloat16),
            pltpu.VMEM((16, TILE, QPK * HEAD_DIM), jnp.bfloat16),
            pltpu.SemaphoreType.DMA((2,)),
            pltpu.SemaphoreType.DMA((2, 2)),
            pltpu.SemaphoreType.DMA((2, 2)),
            pltpu.SemaphoreType.DMA((2, 2)),
            pltpu.SemaphoreType.DMA((12,)),
            pltpu.SemaphoreType.DMA((4, 2, 2)),
            pltpu.SemaphoreType.DMA((4,)),
        ],
        compiler_params=pltpu.CompilerParams(
            collective_id=0, has_side_effects=True, vmem_limit_bytes=48 << 20
        ),
        cost_estimate=pl.CostEstimate(
            flops=flops, bytes_accessed=10 << 20, transcendentals=60 * TILE * width
        ),
    )(tile_docs, queries, keys, values)


def solution(mesh):
    in_specs = (P("tok", "head"), P("tok", "head"), P("tok", "head"), P("tok"))
    out_specs = P(("tok", "head"), None)
    return jax.shard_map(local, mesh=mesh, in_specs=in_specs, out_specs=out_specs, check_vma=False)
```

profile of v0, /device:TPU:102, one launch (start us, length us, event | category | flops | bytes accessed | tf_op | source)
XLA Modules:
  0.0 95.7 jit_solution(3314471496658899751)
XLA Ops:
  0.0 0.0 copy-start
  0.0 1.0 %copy-done = bf16[1024,256]{1,0:T(8,128)(2,1)S(1)} copy-done((bf16[1024,256]{1,0:T(8,128)(2,1)S(1)}, bf16[1024,256]{1,0:T(8,128)(2,1)}, u32[]{:S(2)}) %copy-start) | copy-done | bytes 524312
  1.0 0.0 copy-start.1
  1.0 1.0 %copy-done.1 = bf16[1024,256]{1,0:T(8,128)(2,1)S(1)} copy-done((bf16[1024,256]{1,0:T(8,128)(2,1)S(1)}, bf16[1024,256]{1,0:T(8,128)(2,1)}, u32[]{:S(2)}) %copy-start.1) | copy-done | bytes 524312
  2.1 0.0 copy-start.2
  2.1 0.7 copy-done.2
  2.7 91.0 %shard_map.46 = bf16[256,8192]{1,0:T(8,128)(2,1)S(1)} custom-call(s32[8]{0:T(128)S(1)} %copy-done.2, bf16[1024,2048]{1,0:T(8,128)(2,1)} %q_hbm.1, bf16[1024,256]{1,0:T(8,128)(2,1)S(1)} %copy-done, bf16[1024,256]{1,0:T(8,128)(2,1)S(1)} %copy-done.1), custom_call_target="tpu_custom_call" | custom-call | flops 8053063680 | bytes 10485760 | tf_op jit(solution)/shard_map/pallas_call | solution.py:252
  93.7 2.0 %copy.6 = bf16[256,8192]{1,0:T(8,128)(2,1)} copy(bf16[256,8192]{1,0:T(8,128)(2,1)S(1)} %shard_map.46) | data formatting | bytes 8388608
Async XLA Ops:
  0.0 1.0 %copy-start = (bf16[1024,256]{1,0:T(8,128)(2,1)S(1)}, bf16[1024,256]{1,0:T(8,128)(2,1)}, u32[]{:S(2)}) copy-start(bf16[1024,256]{1,0:T(8,128)(2,1)} %k_hbm.1) | copy-start | bytes 1572868
  1.0 1.0 %copy-start.1 = (bf16[1024,256]{1,0:T(8,128)(2,1)S(1)}, bf16[1024,256]{1,0:T(8,128)(2,1)}, u32[]{:S(2)}) copy-start(bf16[1024,256]{1,0:T(8,128)(2,1)} %v_hbm.1) | copy-start | bytes 1572868
  2.1 0.7 copy-start.2
where the time goes:
time: 95.9 us; the launch traced here: 95.7 us
  Pallas kernels  91 us (95%)
  local copies, waits for them, and re-layouts  4.75 us (5%)
    pallas_call x1, Pallas kernels, local(): pl.pallas_call(kernel, out_shape=jax.ShapeDtypeStruct((rows // heads, wid...  91 us
    unnamed x7, local copies, waits for them, and re-layouts  4.75 us

commit v1 on v0

--- a/solution.py
+++ b/solution.py
@@ -17,8 +17,8 @@
 CHUNK = 256
 
 
-def kernel(docs, q_hbm, k_hbm, v_hbm, out, q, keys, vals, bias, stage,
-           q_sem, kv_sem, rim_send, rim_recv, send_sem, recv_sem, own_sem):
+def kernel(docs_hbm, q_hbm, k_hbm, v_hbm, out, docs, q, keys, vals, bias, stage,
+           docs_sem, q_sem, kv_sem, rim_send, rim_recv, turn, send_sem, recv_sem, own_sem):
     tok, head = lax.axis_index("tok"), lax.axis_index("head")
     y_hi, core = head // 2, head % 2
     odd = tok % 2
@@ -57,6 +57,8 @@
             for which, (here, there) in enumerate(((k_hbm, keys), (v_hbm, vals)))
         ]
 
+    load_docs = pltpu.make_async_copy(docs_hbm, docs, docs_sem)
+    load_docs.start()
     for copy in load_kv(0):
         copy.start()
     load_q(0).start()
@@ -77,11 +79,59 @@
 
     pl.semaphore_wait(barrier, 4)
 
-    @pl.when(odd == 0)
+    def start_rim(g):
+        for copy in rim(g):
+            copy.start()
+
+    def end_rim(g):
+        for copy in rim(g):
+            copy.wait_send()
+
+    def pass_turn():
+        pl.semaphore_signal(turn, inc=1, device_id=sibling, device_id_type=MESH)
+
+    @pl.when((odd == 0) & (core == 0))
     def _():
-        for g in range(2):
-            for copy in rim(g):
-                copy.start()
+        start_rim(0)
+
+    def rim_step(i):
+        @pl.when(core == 0)
+        def _():
+            @pl.when(i == 2)
+            def _():
+                end_rim(0)
+                pass_turn()
+
+            @pl.when(i == 4)
+            def _():
+                pl.semaphore_wait(turn, 1)
+                start_rim(1)
+
+            @pl.when(i == 6)
+            def _():
+                end_rim(1)
+                pass_turn()
+
+        @pl.when(core == 1)
+        def _():
+            @pl.when(i == 2)
+            def _():
+                pl.semaphore_wait(turn, 1)
+                start_rim(0)
+
+            @pl.when(i == 4)
+            def _():
+                end_rim(0)
+                pass_turn()
+
+            @pl.when(i == 6)
+            def _():
+                pl.semaphore_wait(turn, 1)
+                start_rim(1)
+
+            @pl.when(i == 15)
+            def _():
+                end_rim(1)
 
     eye = (
         lax.broadcasted_iota(jnp.int32, (TILE, TILE), 0)
@@ -93,7 +143,7 @@
         span = pl.ds(pl.multiple_of(first * CHUNK, CHUNK), length)
         rows = pl.ds(pl.multiple_of(t * TILE, TILE), TILE)
 
-        def group(j, carry):
+        for j in range(QPK // STACK):
             base = pl.multiple_of((g * QPK + j * STACK) * HEAD_DIM, STACK * HEAD_DIM)
             wide = q[rows, pl.ds(base, STACK * HEAD_DIM)]
             queries = jnp.concatenate(
@@ -117,12 +167,9 @@
                 preferred_element_type=jnp.float32,
             )
             result = (summed[:, :HEAD_DIM] / summed[:, HEAD_DIM:]).astype(jnp.bfloat16)
-            stage[i, :, pl.ds(pl.multiple_of(j * STACK * HEAD_DIM, STACK * HEAD_DIM), STACK * HEAD_DIM)] = (
-                jnp.concatenate([result[a * TILE : (a + 1) * TILE] for a in range(STACK)], 1)
-            )
-            return carry
-
-        lax.fori_loop(0, QPK // STACK, group, 0)
+            stage[i, :, j * STACK * HEAD_DIM : (j + 1) * STACK * HEAD_DIM] = jnp.concatenate(
+                [result[a * TILE : (a + 1) * TILE] for a in range(STACK)], 1
+            )
 
     def place(i):
         crossing = i < 8
@@ -160,6 +207,10 @@
     def unit(i, carry):
         g, t = place(i)
 
+        @pl.when(odd == 0)
+        def _():
+            rim_step(i)
+
         @pl.when(i % 4 == 0)
         def _():
             @pl.when(i < 8)
@@ -174,6 +225,7 @@
 
             @pl.when(i == 0)
             def _():
+                load_docs.wait()
                 load_q(0).wait()
 
             @pl.when(i == 8)
@@ -212,12 +264,6 @@
         return carry
 
     lax.fori_loop(0, 16, unit, 0)
-
-    @pl.when(odd == 0)
-    def _():
-        for g in range(2):
-            for copy in rim(g):
-                copy.wait_send()
 
     def finish(i, carry):
         send(i).wait_send()
@@ -251,25 +297,28 @@
     flops = 2 * 2 * 60 * TILE * TILE * width
     return pl.pallas_call(
         kernel,
-        out_shape=jax.ShapeDtypeStruct((rows // heads, width * heads), jnp.bfloat16),
-        in_specs=[pl.BlockSpec(memory_space=pltpu.SMEM)] + [pl.BlockSpec(memory_space=pl.ANY)] * 3,
+        out_shape=pltpu.VMEM((rows // heads, width * heads), jnp.bfloat16),
+        in_specs=[pl.BlockSpec(memory_space=pltpu.HBM)] * 4,
         out_specs=pl.BlockSpec(memory_space=pl.ANY),
         scratch_shapes=[
+            pltpu.SMEM(tile_docs.shape, jnp.int32),
             pltpu.VMEM((rows, width), jnp.bfloat16),
             pltpu.VMEM((groups, 2 * rows, HEAD_DIM), jnp.bfloat16),
             pltpu.VMEM((groups, 2 * rows, HEAD_DIM), jnp.bfloat16),
             pltpu.VMEM((2 * rows, TILE), jnp.bfloat16),
             pltpu.VMEM((16, TILE, QPK * HEAD_DIM), jnp.bfloat16),
+            pltpu.SemaphoreType.DMA,
             pltpu.SemaphoreType.DMA((2,)),
             pltpu.SemaphoreType.DMA((2, 2)),
             pltpu.SemaphoreType.DMA((2, 2)),
             pltpu.SemaphoreType.DMA((2, 2)),
+            pltpu.SemaphoreType.REGULAR,
             pltpu.SemaphoreType.DMA((12,)),
             pltpu.SemaphoreType.DMA((4, 2, 2)),
             pltpu.SemaphoreType.DMA((4,)),
         ],
         compiler_params=pltpu.CompilerParams(
-            collective_id=0, has_side_effects=True, vmem_limit_bytes=48 << 20
+            collective_id=0, has_side_effects=True, vmem_limit_bytes=59 << 20
         ),
         cost_estimate=pl.CostEstimate(
             flops=flops, bytes_accessed=10 << 20, transcendentals=60 * TILE * width

time: 95.9 us -> 63.1 us (0.66)
  the two profiles are of different devices: /device:TPU:102 before, /device:TPU:127 now
where the time goes in v1:
time: 63.1 us; the launch traced here: 63 us
  Pallas kernels  61 us (97%)
  local copies, waits for them, and re-layouts  2.02 us (3%)
    pallas_call x1, Pallas kernels, local(): pl.pallas_call(kernel, out_shape=pltpu.VMEM((rows // heads, width * heads...  61 us
    unnamed x1, local copies, waits for them, and re-layouts  2.02 us

profile of v1, /device:TPU:127, one launch (start us, length us, event | category | flops | bytes accessed | tf_op | source)
XLA Modules:
  0.0 63.0 jit_solution(1555517121159132516)
XLA Ops:
  0.0 61.0 %shard_map.46 = bf16[256,8192]{1,0:T(8,128)(2,1)S(1)} custom-call(s32[8]{0:T(128)} %docs_hbm.1, bf16[1024,2048]{1,0:T(8,128)(2,1)} %q_hbm.1, bf16[1024,256]{1,0:T(8,128)(2,1)} %k_hbm.1, bf16[1024,256]{1,0:T(8,128)(2,1)} %v_hbm.1), custom_call_target="tpu_custom_call" | custom-call | flops 8053063680 | bytes 10485760 | tf_op jit(solution)/shard_map/pallas_call | solution.py:298
  61.0 2.0 %copy.6 = bf16[256,8192]{1,0:T(8,128)(2,1)} copy(bf16[256,8192]{1,0:T(8,128)(2,1)S(1)} %shard_map.46) | data formatting | bytes 8388608

commit v2 on v1

--- a/solution.py
+++ b/solution.py
@@ -15,10 +15,14 @@
 EXPONENT_SCALE = HEAD_DIM**-0.5 * 1.4426950408889634
 STACK = 2
 CHUNK = 256
-
-
-def kernel(docs_hbm, q_hbm, k_hbm, v_hbm, out, docs, q, keys, vals, bias, stage,
-           docs_sem, q_sem, kv_sem, rim_send, rim_recv, turn, send_sem, recv_sem, own_sem):
+RELAYED = 1
+RELAY_BLOCK = 3
+PIECES = 4
+
+
+def kernel(docs_hbm, q_hbm, k_hbm, v_hbm, out, docs, q, keys, vals, doc_bias, last_bias, stage,
+           docs_sem, q_sem, kv_sem, rim_send, rim_recv, turn, send_sem, recv_sem, own_sem,
+           lent, passed, hop_send, hop_recv):
     tok, head = lax.axis_index("tok"), lax.axis_index("head")
     y_hi, core = head // 2, head % 2
     odd = tok % 2
@@ -94,88 +98,102 @@
     def _():
         start_rim(0)
 
-    def rim_step(i):
+    def rim_step(b):
         @pl.when(core == 0)
         def _():
-            @pl.when(i == 2)
+            @pl.when(b == 1)
             def _():
                 end_rim(0)
                 pass_turn()
 
-            @pl.when(i == 4)
+            @pl.when(b == 2)
             def _():
                 pl.semaphore_wait(turn, 1)
                 start_rim(1)
 
-            @pl.when(i == 6)
+            @pl.when(b == 3)
             def _():
                 end_rim(1)
                 pass_turn()
 
         @pl.when(core == 1)
         def _():
-            @pl.when(i == 2)
+            @pl.when(b == 1)
             def _():
                 pl.semaphore_wait(turn, 1)
                 start_rim(0)
 
-            @pl.when(i == 4)
+            @pl.when(b == 2)
             def _():
                 end_rim(0)
                 pass_turn()
 
-            @pl.when(i == 6)
+            @pl.when(b == 3)
             def _():
                 pl.semaphore_wait(turn, 1)
                 start_rim(1)
 
-            @pl.when(i == 15)
+            @pl.when(b == 7)
             def _():
                 end_rim(1)
 
-    eye = (
-        lax.broadcasted_iota(jnp.int32, (TILE, TILE), 0)
-        == lax.broadcasted_iota(jnp.int32, (TILE, TILE), 1)
-    ).astype(jnp.float32).astype(jnp.bfloat16)
-
-    def attend(i, g, t, first, chunks):
-        length = chunks * CHUNK
-        span = pl.ds(pl.multiple_of(first * CHUNK, CHUNK), length)
-        rows = pl.ds(pl.multiple_of(t * TILE, TILE), TILE)
-
-        for j in range(QPK // STACK):
+    def attend(i, g, parts):
+        items = [(u, j) for u in range(len(parts)) for j in range(QPK // STACK)]
+
+        def reach(u):
+            _, first, chunks = parts[u]
+            return pl.multiple_of(first * CHUNK, CHUNK), chunks * CHUNK
+
+        def score(u, j):
+            at, length = reach(u)
+            rows = pl.ds(pl.multiple_of(parts[u][0] * TILE, TILE), TILE)
             base = pl.multiple_of((g * QPK + j * STACK) * HEAD_DIM, STACK * HEAD_DIM)
             wide = q[rows, pl.ds(base, STACK * HEAD_DIM)]
-            queries = jnp.concatenate(
-                [
-                    jnp.concatenate([wide[:, a * HEAD_DIM : (a + 1) * HEAD_DIM], eye], 1)
-                    for a in range(STACK)
-                ],
-                0,
-            )
-            known = jnp.concatenate([keys[g, span], bias[span]], 1)
             scores = lax.dot_general(
-                queries, known, (((1,), (1,)), ((), ())), preferred_element_type=jnp.float32
-            )
+                jnp.concatenate(
+                    [wide[:, a * HEAD_DIM : (a + 1) * HEAD_DIM] for a in range(STACK)], 0
+                ),
+                keys[g, pl.ds(at, length)],
+                (((1,), (1,)), ((), ())),
+                preferred_element_type=jnp.float32,
+            )
+            body = length - CHUNK
+            tail = scores[:, body:] + jnp.concatenate([last_bias[u]] * STACK, 0)
+            if body == 0:
+                return tail
+            return jnp.concatenate(
+                [scores[:, :body] + doc_bias[u : u + 1, pl.ds(at, body)], tail], 1
+            )
+
+        def finish(u, j, scores):
+            at, length = reach(u)
             maxima = jnp.max(scores, axis=1, keepdims=True)
             weights = jnp.exp2((scores - maxima) * EXPONENT_SCALE).astype(jnp.bfloat16)
             summed = jnp.dot(
                 weights,
                 jnp.concatenate(
-                    [vals[g, span], jnp.ones((length, HEAD_DIM), jnp.bfloat16)], 1
+                    [vals[g, pl.ds(at, length)], jnp.ones((length, HEAD_DIM), jnp.bfloat16)], 1
                 ),
                 preferred_element_type=jnp.float32,
             )
             result = (summed[:, :HEAD_DIM] / summed[:, HEAD_DIM:]).astype(jnp.bfloat16)
-            stage[i, :, j * STACK * HEAD_DIM : (j + 1) * STACK * HEAD_DIM] = jnp.concatenate(
+            stage[i + u, :, j * STACK * HEAD_DIM : (j + 1) * STACK * HEAD_DIM] = jnp.concatenate(
                 [result[a * TILE : (a + 1) * TILE] for a in range(STACK)], 1
             )
+
+        scores = score(*items[0])
+        for n, item in enumerate(items):
+            ahead = score(*items[n + 1]) if n + 1 < len(items) else None
+            finish(*item, scores)
+            scores = ahead
+            if item == (0, QPK // STACK - 1):
+                dispatch(i)
 
     def place(i):
         crossing = i < 8
         g = jnp.where(crossing, i // 4, (i // 2) % 2)
         t = jnp.where(
-            crossing, far + i % 4, near + 2 * jnp.where(i < 12, 1 - core, core) + i % 2
+            crossing, far + (i + 2 * core) % 4, near + 2 * jnp.where(i < 12, 1 - core, core) + i % 2
         )
         return g, t
 
@@ -204,69 +222,113 @@
             own_sem.at[i - 12],
         )
 
-    def unit(i, carry):
-        g, t = place(i)
+    def hop(n, p):
+        rows = pl.ds(p * (TILE // PIECES), TILE // PIECES)
+        opposite = (tok, (head + 2) % 4)
+        column = pl.multiple_of((head + 2) % 4 * 2 * QPK * HEAD_DIM, QPK * HEAD_DIM)
+        source, target, device = (
+            (stage.at[RELAYED, rows], lent.at[rows], neighbour),
+            (lent.at[rows], passed.at[rows], opposite),
+            (
+                passed.at[rows],
+                out.at[
+                    pl.ds(TILE + p * (TILE // PIECES), TILE // PIECES),
+                    pl.ds(column, QPK * HEAD_DIM),
+                ],
+                neighbour,
+            ),
+        )[n]
+        return pltpu.make_async_remote_copy(
+            src_ref=source, dst_ref=target, send_sem=hop_send.at[n, p], recv_sem=hop_recv.at[n, p],
+            device_id=device, device_id_type=MESH,
+        )
+
+    def dispatch(i):
+        relayed = (odd == 1) & (i == RELAYED)
+
+        @pl.when((i < 12) & jnp.logical_not(relayed))
+        def _():
+            send(i).start()
+
+        @pl.when(relayed)
+        def _():
+            for p in range(PIECES):
+                hop(0, p).start()
+
+        @pl.when(i >= 12)
+        def _():
+            keep(i).start()
+
+    def block(b, carry):
+        i = 2 * b
+        g = place(i)[0]
 
         @pl.when(odd == 0)
         def _():
-            rim_step(i)
-
-        @pl.when(i % 4 == 0)
-        def _():
-            @pl.when(i < 8)
-            def _():
-                for copy in load_kv(i // 4):
-                    copy.wait()
-
-                @pl.when(odd == 1)
-                def _():
-                    for copy in rim(i // 4):
-                        copy.wait_recv()
-
-            @pl.when(i == 0)
-            def _():
-                load_docs.wait()
-                load_q(0).wait()
-
-            @pl.when(i == 8)
-            def _():
-                load_q(1).wait()
-
-        reaches_back = jnp.where(t == 7, 0, odd)
-        first = 3 - 3 * reaches_back
-        count = (7 + t) // 2 + 1 - first
-        begin = (docs[t] - 8 * tok + 7) * TILE
-        row = lax.broadcasted_iota(jnp.int32, (CHUNK, TILE), 1) + (7 + t) * TILE
-
-        def hide(c, carry):
-            at = pl.multiple_of((first + c) * CHUNK, CHUNK)
-            key = lax.broadcasted_iota(jnp.int32, (CHUNK, TILE), 0) + at
-            bias[pl.ds(at, CHUNK)] = jnp.where(
-                (key >= begin) & (key <= row), 0.0, HIDDEN
-            ).astype(jnp.bfloat16)
-            return carry
-
-        lax.fori_loop(0, count, hide, 0)
-
-        for chunks in range(1, 8):
-            @pl.when(count == chunks)
-            def _(chunks=chunks):
-                attend(i, g, t, first, chunks)
-
-        @pl.when(i < 12)
-        def _():
-            send(i).start()
-
-        @pl.when(i >= 12)
-        def _():
-            keep(i).start()
+            rim_step(b)
+
+        @pl.when((b == RELAY_BLOCK) & (odd == 0))
+        def _():
+            for p in range(PIECES):
+                hop(0, p).wait_recv()
+                hop(1, p).start()
+
+        @pl.when((b == 0) | (b == 2))
+        def _():
+            for copy in load_kv(b // 2):
+                copy.wait()
+
+            @pl.when(odd == 1)
+            def _():
+                for copy in rim(b // 2):
+                    copy.wait_recv()
+
+        @pl.when(b == 0)
+        def _():
+            load_docs.wait()
+            load_q(0).wait()
+
+        @pl.when(b == 4)
+        def _():
+            load_q(1).wait()
+
+        parts = []
+        for u in range(2):
+            t = place(i + u)[1]
+            reaches_back = jnp.where(t == 7, 0, odd)
+            first = 3 - 3 * reaches_back
+            count = (7 + t) // 2 + 1 - first
+            begin = (docs[t] - 8 * tok + 7) * TILE
+            doc_bias[u : u + 1, :] = jnp.where(
+                lax.broadcasted_iota(jnp.int32, (1, doc_bias.shape[1]), 1) >= begin, 0.0, HIDDEN
+            )
+            key = lax.broadcasted_iota(jnp.int32, (TILE, CHUNK), 1) + (first + count - 1) * CHUNK
+            row = lax.broadcasted_iota(jnp.int32, (TILE, CHUNK), 0) + (7 + t) * TILE
+            last_bias[u] = jnp.where((key >= begin) & (key <= row), 0.0, HIDDEN)
+            parts.append((t, first, count))
+
+        for counts in ((1, 2), (2, 3), (3, 4), (4, 5), (5, 6), (6, 7), (7, 5)):
+            @pl.when(parts[0][2] == counts[0])
+            def _(counts=counts):
+                attend(i, g, [(t, first, n) for (t, first, _), n in zip(parts, counts)])
+
+        dispatch(i + 1)
 
         return carry
 
-    lax.fori_loop(0, 16, unit, 0)
+    lax.fori_loop(0, 8, block, 0)
+
+    @pl.when(odd == 0)
+    def _():
+        for p in range(PIECES):
+            hop(1, p).wait_recv()
+            hop(2, p).start()
 
     def finish(i, carry):
-        send(i).wait_send()
+        @pl.when((odd == 0) | (i != RELAYED))
+        def _():
+            send(i).wait_send()
+
         return carry
 
     lax.fori_loop(0, 12, finish, 0)
@@ -280,13 +342,29 @@
             pl.ds(pl.multiple_of(half * TILE, TILE), TILE),
             pl.ds(pl.multiple_of((other * 2 + g) * QPK * HEAD_DIM, QPK * HEAD_DIM), QPK * HEAD_DIM),
         ]
-        pltpu.make_async_remote_copy(
-            src_ref=stage.at[0], dst_ref=piece, send_sem=send_sem.at[0],
-            recv_sem=recv_sem.at[other, g, half], device_id=sibling, device_id_type=MESH,
-        ).wait_recv()
+
+        @pl.when((odd == 0) | (n != 5))
+        def _():
+            pltpu.make_async_remote_copy(
+                src_ref=stage.at[0], dst_ref=piece, send_sem=send_sem.at[0],
+                recv_sem=recv_sem.at[other, g, half], device_id=sibling, device_id_type=MESH,
+            ).wait_recv()
+
         return carry
 
     lax.fori_loop(0, 12, arrive, 0)
+
+    @pl.when(odd == 0)
+    def _():
+        for p in range(PIECES):
+            hop(1, p).wait_send()
+            hop(2, p).wait_send()
+
+    @pl.when(odd == 1)
+    def _():
+        for p in range(PIECES):
+            hop(0, p).wait_send()
+            hop(2, p).wait_recv()
 
 
 def local(queries, keys, values, tile_docs):
@@ -305,7 +383,8 @@
             pltpu.VMEM((rows, width), jnp.bfloat16),
             pltpu.VMEM((groups, 2 * rows, HEAD_DIM), jnp.bfloat16),
             pltpu.VMEM((groups, 2 * rows, HEAD_DIM), jnp.bfloat16),
-            pltpu.VMEM((2 * rows, TILE), jnp.bfloat16),
+            pltpu.VMEM((8, 2 * rows), jnp.float32),
+            pltpu.VMEM((2, TILE, CHUNK), jnp.float32),
             pltpu.VMEM((16, TILE, QPK * HEAD_DIM), jnp.bfloat16),
             pltpu.SemaphoreType.DMA,
             pltpu.SemaphoreType.DMA((2,)),
@@ -316,6 +395,10 @@
             pltpu.SemaphoreType.DMA((12,)),
             pltpu.SemaphoreType.DMA((4, 2, 2)),
             pltpu.SemaphoreType.DMA((4,)),
+            pltpu.VMEM((TILE, QPK * HEAD_DIM), jnp.bfloat16),
+            pltpu.VMEM((TILE, QPK * HEAD_DIM), jnp.bfloat16),
+            pltpu.SemaphoreType.DMA((3, PIECES)),
+            pltpu.SemaphoreType.DMA((3, PIECES)),
         ],
         compiler_params=pltpu.CompilerParams(
             collective_id=0, has_side_effects=True, vmem_limit_bytes=59 << 20

time: 63.1 us -> 60.9 us (0.965)
  the two profiles are of different devices: /device:TPU:127 before, /device:TPU:1 now
where the time goes in v2:
time: 60.9 us; the launch traced here: 60.8 us
  Pallas kernels  58.8 us (97%)
  local copies, waits for them, and re-layouts  2.02 us (3%)
    pallas_call x1, Pallas kernels, local(): pl.pallas_call(kernel, out_shape=pltpu.VMEM((rows // heads, width * heads...  58.8 us
    unnamed x1, local copies, waits for them, and re-layouts  2.02 us

profile of v2, /device:TPU:1, one launch (start us, length us, event | category | flops | bytes accessed | tf_op | source)
XLA Modules:
  0.0 60.8 jit_solution(17708391689089650274)
XLA Ops:
  0.0 58.8 %shard_map.46 = bf16[256,8192]{1,0:T(8,128)(2,1)S(1)} custom-call(s32[8]{0:T(128)} %docs_hbm.1, bf16[1024,2048]{1,0:T(8,128)(2,1)} %q_hbm.1, bf16[1024,256]{1,0:T(8,128)(2,1)} %k_hbm.1, bf16[1024,256]{1,0:T(8,128)(2,1)} %v_hbm.1), custom_call_target="tpu_custom_call" | custom-call | flops 8053063680 | bytes 10485760 | tf_op jit(solution)/shard_map/pallas_call | solution.py:376
  58.8 2.0 %copy.6 = bf16[256,8192]{1,0:T(8,128)(2,1)} copy(bf16[256,8192]{1,0:T(8,128)(2,1)S(1)} %shard_map.46) | data formatting | bytes 8388608

commit v3 on v2

--- a/solution.py
+++ b/solution.py
@@ -15,9 +15,10 @@
 EXPONENT_SCALE = HEAD_DIM**-0.5 * 1.4426950408889634
 STACK = 2
 CHUNK = 256
-RELAYED = 1
 RELAY_BLOCK = 3
-PIECES = 4
+PIECES = 3
+KEPT = 32
+PIECE = (TILE - KEPT) // PIECES
 
 
 def kernel(docs_hbm, q_hbm, k_hbm, v_hbm, out, docs, q, keys, vals, doc_bias, last_bias, stage,
@@ -37,8 +38,10 @@
     far, near = 4 * (1 - y_hi), 4 * y_hi
 
     def load_q(part):
-        first = pl.multiple_of(jnp.where(part == 0, far, near) * TILE, 4 * TILE)
-        rows = pl.ds(first, 4 * TILE)
+        first, tiles = (
+            (far + 2 * odd, 2), (far + 2 - 2 * odd, 2), (near, 4)
+        )[part]
+        rows = pl.ds(pl.multiple_of(first * TILE, 2 * TILE), tiles * TILE)
         return pltpu.make_async_copy(q_hbm.at[rows], q.at[rows], q_sem.at[part])
 
     def load_kv(g):
@@ -66,9 +69,10 @@
     for copy in load_kv(0):
         copy.start()
     load_q(0).start()
+    load_q(1).start()
     for copy in load_kv(1):
         copy.start()
-    load_q(1).start()
+    load_q(2).start()
 
     blank = jnp.zeros((TILE, HEAD_DIM), jnp.bfloat16)
     for g in range(2):
@@ -193,16 +197,16 @@
         crossing = i < 8
         g = jnp.where(crossing, i // 4, (i // 2) % 2)
         t = jnp.where(
-            crossing, far + (i + 2 * core) % 4, near + 2 * jnp.where(i < 12, 1 - core, core) + i % 2
+            crossing, far + (i + 2 * odd) % 4, near + 2 * jnp.where(i < 12, 1 - core, core) + i % 2
         )
         return g, t
 
-    def send(i):
+    def send(i, rows=TILE):
         g, t = place(i)
         return pltpu.make_async_remote_copy(
-            src_ref=stage.at[i],
+            src_ref=stage.at[i, pl.ds(0, rows)],
             dst_ref=out.at[
-                pl.ds(pl.multiple_of((t % 2) * TILE, TILE), TILE),
+                pl.ds(pl.multiple_of((t % 2) * TILE, TILE), rows),
                 pl.ds(pl.multiple_of((head * 2 + g) * QPK * HEAD_DIM, QPK * HEAD_DIM), QPK * HEAD_DIM),
             ],
             send_sem=send_sem.at[i],
@@ -222,17 +226,19 @@
             own_sem.at[i - 12],
         )
 
+    relay_unit = 3 - 2 * core
+
     def hop(n, p):
-        rows = pl.ds(p * (TILE // PIECES), TILE // PIECES)
+        rows = pl.ds(KEPT + p * PIECE, PIECE)
         opposite = (tok, (head + 2) % 4)
         column = pl.multiple_of((head + 2) % 4 * 2 * QPK * HEAD_DIM, QPK * HEAD_DIM)
         source, target, device = (
-            (stage.at[RELAYED, rows], lent.at[rows], neighbour),
+            (stage.at[relay_unit, rows], lent.at[rows], neighbour),
             (lent.at[rows], passed.at[rows], opposite),
             (
                 passed.at[rows],
                 out.at[
-                    pl.ds(TILE + p * (TILE // PIECES), TILE // PIECES),
+                    pl.ds(TILE + KEPT + p * PIECE, PIECE),
                     pl.ds(column, QPK * HEAD_DIM),
                 ],
                 neighbour,
@@ -244,7 +250,7 @@
         )
 
     def dispatch(i):
-        relayed = (odd == 1) & (i == RELAYED)
+        relayed = (odd == 1) & (i == relay_unit)
 
         @pl.when((i < 12) & jnp.logical_not(relayed))
         def _():
@@ -252,6 +258,7 @@
 
         @pl.when(relayed)
         def _():
+            send(i, KEPT).start()
             for p in range(PIECES):
                 hop(0, p).start()
 
@@ -288,9 +295,13 @@
             load_docs.wait()
             load_q(0).wait()
 
+        @pl.when(b == 1)
+        def _():
+            load_q(1).wait()
+
         @pl.when(b == 4)
         def _():
-            load_q(1).wait()
+            load_q(2).wait()
 
         parts = []
         for u in range(2):
@@ -325,9 +336,15 @@
             hop(2, p).start()
 
     def finish(i, carry):
-        @pl.when((odd == 0) | (i != RELAYED))
+        relayed = (odd == 1) & (i == relay_unit)
+
+        @pl.when(jnp.logical_not(relayed))
         def _():
             send(i).wait_send()
+
+        @pl.when(relayed)
+        def _():
+            send(i, KEPT).wait_send()
 
         return carry
 
@@ -338,17 +355,29 @@
     def arrive(n, carry):
         other = (head + 1 + n // 4) % 4
         g, half = (n // 2) % 2, n % 2
-        piece = out.at[
-            pl.ds(pl.multiple_of(half * TILE, TILE), TILE),
-            pl.ds(pl.multiple_of((other * 2 + g) * QPK * HEAD_DIM, QPK * HEAD_DIM), QPK * HEAD_DIM),
-        ]
-
-        @pl.when((odd == 0) | (n != 5))
-        def _():
-            pltpu.make_async_remote_copy(
-                src_ref=stage.at[0], dst_ref=piece, send_sem=send_sem.at[0],
-                recv_sem=recv_sem.at[other, g, half], device_id=sibling, device_id_type=MESH,
-            ).wait_recv()
+
+        def arrival(rows):
+            return pltpu.make_async_remote_copy(
+                src_ref=stage.at[0, pl.ds(0, rows)],
+                dst_ref=out.at[
+                    pl.ds(pl.multiple_of(half * TILE, TILE), rows),
+                    pl.ds(pl.multiple_of((other * 2 + g) * QPK * HEAD_DIM, QPK * HEAD_DIM), QPK * HEAD_DIM),
+                ],
+                send_sem=send_sem.at[0],
+                recv_sem=recv_sem.at[other, g, half],
+                device_id=sibling,
+                device_id_type=MESH,
+            )
+
+        relayed = (odd == 1) & (n == 5)
+
+        @pl.when(jnp.logical_not(relayed))
+        def _():
+            arrival(TILE).wait_recv()
+
+        @pl.when(relayed)
+        def _():
+            arrival(KEPT).wait_recv()
 
         return carry
 
@@ -387,7 +416,7 @@
             pltpu.VMEM((2, TILE, CHUNK), jnp.float32),
             pltpu.VMEM((16, TILE, QPK * HEAD_DIM), jnp.bfloat16),
             pltpu.SemaphoreType.DMA,
-            pltpu.SemaphoreType.DMA((2,)),
+            pltpu.SemaphoreType.DMA((3,)),
             pltpu.SemaphoreType.DMA((2, 2)),
             pltpu.SemaphoreType.DMA((2, 2)),
             pltpu.SemaphoreType.DMA((2, 2)),

time: 60.9 us -> 59.1 us (0.970)
  Pallas kernels: 58.8 us -> 56.6 us
    pallas_call x1, Pallas kernels: 58.8 us -> 56.6 us  [local(): pl.pallas_call(kernel, out_shape=pltpu.VMEM((rows // heads, width * heads...]
where the time goes in v3:
time: 59.1 us; the launch traced here: 58.6 us
  Pallas kernels  56.6 us (96%)
  local copies, waits for them, and re-layouts  2.02 us (3%)
    pallas_call x1, Pallas kernels, local(): pl.pallas_call(kernel, out_shape=pltpu.VMEM((rows // heads, width * heads...  56.6 us
    unnamed x1, local copies, waits for them, and re-layouts  2.02 us

profile of v3, /device:TPU:1, one launch (start us, length us, event | category | flops | bytes accessed | tf_op | source)
XLA Modules:
  0.0 58.6 jit_solution(809559859993401893)
XLA Ops:
  0.0 56.6 %shard_map.46 = bf16[256,8192]{1,0:T(8,128)(2,1)S(1)} custom-call(s32[8]{0:T(128)} %docs_hbm.1, bf16[1024,2048]{1,0:T(8,128)(2,1)} %q_hbm.1, bf16[1024,256]{1,0:T(8,128)(2,1)} %k_hbm.1, bf16[1024,256]{1,0:T(8,128)(2,1)} %v_hbm.1), custom_call_target="tpu_custom_call" | custom-call | flops 8053063680 | bytes 10485760 | tf_op jit(solution)/shard_map/pallas_call | solution.py:405
  56.6 2.0 %copy.6 = bf16[256,8192]{1,0:T(8,128)(2,1)} copy(bf16[256,8192]{1,0:T(8,128)(2,1)S(1)} %shard_map.46) | data formatting | bytes 8388608

commit v4 on v3

--- a/solution.py
+++ b/solution.py
@@ -141,6 +141,13 @@
             def _():
                 end_rim(1)
 
+    def ready(g, which):
+        load_kv(g)[which].wait()
+
+        @pl.when(odd == 1)
+        def _():
+            rim(g)[which].wait_recv()
+
     def attend(i, g, parts):
         items = [(u, j) for u in range(len(parts)) for j in range(QPK // STACK)]
 
@@ -188,6 +195,10 @@
         scores = score(*items[0])
         for n, item in enumerate(items):
             ahead = score(*items[n + 1]) if n + 1 < len(items) else None
+            if n == 0:
+                @pl.when((i == 0) | (i == 4))
+                def _():
+                    ready(i // 4, 1)
             finish(*item, scores)
             scores = ahead
             if item == (0, QPK // STACK - 1):
@@ -282,13 +293,7 @@
 
         @pl.when((b == 0) | (b == 2))
         def _():
-            for copy in load_kv(b // 2):
-                copy.wait()
-
-            @pl.when(odd == 1)
-            def _():
-                for copy in rim(b // 2):
-                    copy.wait_recv()
+            ready(b // 2, 0)
 
         @pl.when(b == 0)
         def _():

time: 59.1 us -> 58.8 us (level)
  no operation moved by 1% of the time
where the time goes in v4:
time: 58.8 us; the launch traced here: 58.7 us
  Pallas kernels  56.7 us (96%)
  local copies, waits for them, and re-layouts  2.02 us (3%)
    pallas_call x1, Pallas kernels, local(): pl.pallas_call(kernel, out_shape=pltpu.VMEM((rows // heads, width * heads...  56.7 us
    unnamed x1, local copies, waits for them, and re-layouts  2.02 us

profile of v4, /device:TPU:1, one launch (start us, length us, event | category | flops | bytes accessed | tf_op | source)
XLA Modules:
  0.0 58.7 jit_solution(3467306177402933996)
XLA Ops:
  0.0 56.7 %shard_map.46 = bf16[256,8192]{1,0:T(8,128)(2,1)S(1)} custom-call(s32[8]{0:T(128)} %docs_hbm.1, bf16[1024,2048]{1,0:T(8,128)(2,1)} %q_hbm.1, bf16[1024,256]{1,0:T(8,128)(2,1)} %k_hbm.1, bf16[1024,256]{1,0:T(8,128)(2,1)} %v_hbm.1), custom_call_target="tpu_custom_call" | custom-call | flops 8053063680 | bytes 10485760 | tf_op jit(solution)/shard_map/pallas_call | solution.py:410
  56.7 2.0 %copy.6 = bf16[256,8192]{1,0:T(8,128)(2,1)} copy(bf16[256,8192]{1,0:T(8,128)(2,1)S(1)} %shard_map.46) | data formatting | bytes 8388608
